TPU v7x, 32 devices: a whole 2x2x4 slice. The times are simulated.
32 devices in a mesh: dp: 2 (over x), expert: 4 (over y, core), mp: 4 (over z).
Axes of the slice: x: 2, y: 2, z: 4, core: 2. Of those that a mesh axis runs over, the one named last changes fastest.
Arguments:
- tokens: bfloat16 [128, 3072], P('dp'), may hold values from -6 to 6
- expert_ids: int32 [128, 2], P('dp'), may hold values from 0 to 3, all different within a row; in each aligned block of 64 rows (0 to 63, 64 to 127, ...) at most 64 rows name the same one
- gate_values: float32 [128, 2], P('dp'), may hold values from 0.2 to 1
- targets: int32 [128], P('dp'), may hold values from 0 to 32767
- w_gate: bfloat16 [4, 3072, 4, 2048], P('expert', None, 'mp', 'dp'), may hold values from -0.109375 to 0.109375
- w_up: bfloat16 [4, 3072, 4, 2048], P('expert', None, 'mp', 'dp'), may hold values from -0.109375 to 0.109375
- w_down: bfloat16 [4, 4, 2048, 3072], P('expert', 'mp', None, 'dp'), may hold values from -0.0625 to 0.0625
- norm_gain: float32 [3072], replicated, may hold values from 0.1 to 1.9
- lens_head: bfloat16 [3072, 32768], P('dp', ('expert', 'mp')), may hold values from -120 to 120
Outputs:
- mixed: bfloat16 [128, 3072], P('dp')
- log_probs: float32 [128], P('dp')
Inputs may be any that keep to these rules, and one draw needn't show every extreme that they name: `expert_ids`: each row names two different experts; in each aligned block of 64 rows no expert is named by more than 64 rows, a bound that some block reaches.
All inputs are finite; a program needn't handle non-finite values.
Results may differ from a plain program's by a relative error of at most 0.0041.
Values may be sent and summed in bfloat16 or wider, within the bound.
A program may use at most 128 MiB of HBM per device.

v0:
```python
import jax
import jax.numpy as jnp
from jax import lax
from jax.sharding import PartitionSpec as P

f32, bf16 = (jnp.float32, jnp.bfloat16)


def per_device(
    tokens, expert_ids, gate_values, targets, w_gate, w_up, w_down, norm_gain, lens_head
):
    rows, feats = tokens.shape
    owner = lax.axis_index("expert")
    weights = jnp.sum(jnp.where(expert_ids == owner, gate_values, f32(0.0)), axis=1)
    gate_mat = w_gate.reshape(feats, -1)
    up_mat = w_up.reshape(feats, -1)
    down_mat = w_down.reshape(w_down.shape[2], w_down.shape[3])
    own_feats = down_mat.shape[1]
    all_tokens = lax.all_gather(tokens, "dp", axis=0, tiled=True)
    all_weights = lax.all_gather(weights, "dp", axis=0, tiled=True)
    gate_part = jnp.dot(all_tokens, gate_mat, preferred_element_type=f32)
    up_part = jnp.dot(all_tokens, up_mat, preferred_element_type=f32)
    hidden = (jax.nn.silu(gate_part) * up_part).astype(bf16)
    hidden = lax.all_gather(hidden, "dp", axis=1, tiled=True)
    part = jnp.dot(hidden, down_mat, preferred_element_type=f32) * all_weights[:, None]
    summed = lax.psum(part, ("expert", "mp"))
    first = lax.axis_index("dp") * own_feats
    own_tokens = lax.dynamic_slice_in_dim(all_tokens, first, own_feats, axis=1)
    own_gain = lax.dynamic_slice_in_dim(norm_gain, first, own_feats, axis=0)
    mixed_part = (own_tokens.astype(f32) + summed).astype(bf16)
    mixed = lax.all_to_all(mixed_part, "dp", split_axis=0, concat_axis=1, tiled=True)
    mixed_f = mixed.astype(f32)
    scale = lax.rsqrt(jnp.mean(mixed_f * mixed_f, axis=1) + 1e-05)
    gained = (mixed_part.astype(f32) * own_gain[None, :]).astype(bf16)
    logits_part = jnp.dot(gained, lens_head, preferred_element_type=f32)
    logits = lax.psum_scatter(logits_part, "dp", scatter_dimension=0, tiled=True)
    logits = logits * scale[:, None]
    vocab_cols = lens_head.shape[1]
    vocab_start = (owner * lax.axis_size("mp") + lax.axis_index("mp")) * vocab_cols
    columns = vocab_start + lax.broadcasted_iota(jnp.int32, (1, vocab_cols), 1)
    hit = columns == targets[:, None]
    target_local = jnp.sum(jnp.where(hit, logits, f32(0.0)), axis=1)
    top = jnp.max(logits, axis=1)
    total = jnp.sum(jnp.exp(logits - top[:, None]), axis=1)
    stats = lax.all_gather(jnp.stack([top, total, target_local]), ("expert", "mp"))
    tops, totals, hits = (stats[:, 0], stats[:, 1], stats[:, 2])
    top_all = jnp.max(tops, axis=0)
    exp_total = jnp.sum(totals * jnp.exp(tops - top_all[None, :]), axis=0)
    log_probs = jnp.sum(hits, axis=0) - top_all - jnp.log(exp_total)
    return (mixed, log_probs)


def solution(mesh):
    in_specs = (
        P("dp", None),
        P("dp", None),
        P("dp", None),
        P("dp"),
        P("expert", None, "mp", "dp"),
        P("expert", None, "mp", "dp"),
        P("expert", "mp", None, "dp"),
        P(),
        P("dp", ("expert", "mp")),
    )
    out_specs = (P("dp", None), P("dp"))
    return jax.shard_map(
        per_device, mesh=mesh, in_specs=in_specs, out_specs=out_specs, check_vma=False
    )
```

profile of v0, /device:TPU:0, one launch (start us, length us, event | category | flops | bytes accessed | tf_op | source)
XLA Modules:
  0.0 207.5 jit_solution(1650163457520954662)
XLA Ops:
  7.2 0.0 all-reduce.3.cloned.1.call-start
  7.2 0.0 slice-start
  7.2 13.1 %all_gather.15 = bf16[128,3072]{1,0:T(8,128)(2,1)S(1)} all-gather(bf16[64,3072]{1,0:T(8,128)(2,1)} %param.9), channel_id=1, replica_groups=mesh['dp'=2,'expert'=4,'mp'=4] {'dp'}, dimensions={0}, use_global_device_ids=true | all-gather | bytes 1179648 | tf_op jit(solution)/shard_map/all_gather | solution.py:19
  20.3 3.9 %fusion.4 = f32[128,1024]{1,0:T(8,128)S(1)} fusion(bf16[128,3072]{1,0:T(8,128)(2,1)S(1)} %all_gather.15, bf16[1,3072,1,1024]{3,1,2,0:T(8,128)(2,1)} %param.13), kind=kOutput, calls=%fused_computation.4 | convolution fusion | flops 805306368 | bytes 7602176 | tf_op jit(solution)/shard_map/dot_general | solution.py:21
  24.2 0.0 slice-done
  24.2 0.0 slice-done.1
  24.3 0.0 copy-start.4
  24.3 0.0 copy-start.1
  24.3 0.0 copy-start.2
  24.3 1.1 fusion.12
  25.4 8.2 %all_gather.16 = bf16[128,2048]{1,0:T(8,128)(2,1)S(1)} all-gather(bf16[128,1024]{1,0:T(8,128)(2,1)S(1)} %fusion.12), channel_id=1, replica_groups=mesh['dp'=2,'expert'=4,'mp'=4] {'dp'}, dimensions={1}, use_global_device_ids=true | all-gather | bytes 786432 | tf_op jit(solution)/shard_map/all_gather | solution.py:24
  33.6 0.0 copy-done.4
  33.6 0.6 dynamic-slice
  34.9 0.2 dynamic-update-slice
  35.1 4.9 %all-reduce = f32[128]{0:T(128)S(1)} all-reduce(f32[128]{0:T(128)S(1)} %dynamic-update-slice), channel_id=1, replica_groups=mesh['dp'=2,'expert'=4,'mp'=4] {'dp'}, use_global_device_ids=true, to_apply=%add | all-reduce | flops 128 | bytes 1024
  40.0 4.7 %fusion.6 = f32[128,1536]{1,0:T(8,128)} fusion(bf16[128,2048]{1,0:T(8,128)(2,1)S(1)} %all_gather.16, bf16[1,1,2048,1536]{3,2,1,0:T(8,128)(2,1)} %param.15, f32[128]{0:T(128)S(1)} %all-reduce), kind=kOutput, calls=%fused_computation.6 | convolution fusion | flops 805502976 | bytes 7602688 | tf_op jit(solution)/shard_map/dot_general | solution.py:25
  44.7 0.0 all-reduce.3.cloned.1.call-update
  44.7 0.0 reduce-scatter.2.cloned.1.call-start
  44.8 0.1 dynamic_slice.7
  44.9 93.2 %all-reduce.3.cloned.1.call-done = f32[128,1536]{1,0:T(8,128)} async-done(((f32[128,1536]{1,0:T(8,128)}), f32[128,1536]{1,0:T(8,128)}) %all-reduce.3.cloned.1.call-update) | async-done | bytes 786448 | tf_op jit(solution)/shard_map/psum | solution.py:26
  138.1 1.9 add_convert_fusion
  140.0 4.9 %fusion.15 = f32[128,2048]{1,0:T(8,128)} fusion(bf16[1536,2048]{1,0:T(8,128)(2,1)} %param.17, bf16[128,1536]{1,0:T(8,128)(2,1)} %add_convert_fusion, f32[1536]{0:T(1024)S(1)} %dynamic_slice.7), kind=kOutput, calls=%fused_computation.15 | convolution fusion | flops 805896192 | bytes 7739392 | tf_op jit(solution)/shard_map/dot_general | solution.py:35
  144.9 0.0 reduce-scatter.2.cloned.1.call-update
  145.0 3.5 %all-to-all-start = ((bf16[2,64,1536]{2,1,0:T(8,128)(2,1)}), bf16[2,64,1536]{2,1,0:T(8,128)(2,1)S(1)}, u32[]{:S(2)}, u32[]{:S(2)}) async-start(bf16[2,64,1536]{2,1,0:T(8,128)(2,1)} %bitcast.4), calls=%async_computation | async-start | bytes 786432 | tf_op jit(solution)/shard_map/all_to_all | solution.py:31
  148.5 10.2 %all-to-all-done = bf16[2,64,1536]{2,1,0:T(8,128)(2,1)S(1)} async-done(((bf16[2,64,1536]{2,1,0:T(8,128)(2,1)}), bf16[2,64,1536]{2,1,0:T(8,128)(2,1)S(1)}, u32[]{:S(2)}, u32[]{:S(2)}) %all-to-all-start) | async-done | bytes 393248 | tf_op jit(solution)/shard_map/all_to_all | solution.py:31
  158.6 0.8 copy.16
  159.4 0.2 multiply_reduce_fusion
  159.6 7.2 %reduce-scatter.2.cloned.1.call-done = f32[64,2048]{1,0:T(8,128)} async-done(((f32[128,2048]{1,0:T(8,128)}), f32[64,2048]{1,0:T(8,128)}) %reduce-scatter.2.cloned.1.call-update) | async-done | bytes 524304 | tf_op jit(solution)/shard_map/reduce_scatter | solution.py:36
  166.8 1.2 multiply_reduce_fusion.1
  168.0 1.4 exponential_reduce_fusion
  169.4 30.6 %all-gather.1 = f32[16,3,64]{2,1,0:T(4,128)S(1)} all-gather(f32[1,3,64]{2,1,0:T(4,128)S(1)} %maximum_bitcast_fusion), channel_id=2, replica_groups=mesh['dp'=2,'expert'=4,'mp'=4] {'expert','mp'}, dimensions={0}, use_global_device_ids=true | all-gather | bytes 13056 | tf_op jit(solution)/shard_map/all_gather | solution.py:45
  200.1 0.5 log_subtract_fusion
  (15 shorter events, 0.1 us)
Async XLA Ops:
  7.2 130.9 %all-reduce.3.cloned.1.call-start = ((), (), s32[]{:S(2)}) async-start(), calls=%async_computation.2 | async-start | bytes 1572864 | tf_op jit(solution)/shard_map/psum | solution.py:26
  7.2 17.0 %slice-start = ((s8[6291456]{0:T(1024)(128)(4,1)}), s8[4194304]{0:T(1024)(128)(4,1)S(1)}, s32[]{:S(2)}) async-start(s8[6291456]{0:T(1024)(128)(4,1)} %bitcast.41), calls=%async_computation.4 | async-start | bytes 8388608
  20.3 3.9 %slice-start.1 = ((s8[6291456]{0:T(1024)(128)(4,1)}), s8[2097152]{0:T(1024)(128)(4,1)S(1)}, s32[]{:S(2)}) async-start(s8[6291456]{0:T(1024)(128)(4,1)} %bitcast.41), calls=%async_computation.5 | async-start | bytes 4194304
  24.3 9.3 %copy-start.4 = (u32[32]{0:T(128)S(1)}, u32[32]{0:T(128)}, u32[]{:S(2)}) copy-start(u32[32]{0:T(128)} %constant.40) | copy-start | bytes 388
  24.3 10.5 %copy-start.1 = (f32[64,2]{0,1:T(2,128)S(1)}, f32[64,2]{0,1:T(2,128)}, u32[]{:S(2)}) copy-start(f32[64,2]{0,1:T(2,128)} %param.11) | copy-start | bytes 1540
  24.3 10.5 %copy-start.2 = (s32[64,2]{0,1:T(2,128)S(1)}, s32[64,2]{0,1:T(2,128)}, u32[]{:S(2)}) copy-start(s32[64,2]{0,1:T(2,128)} %param.10) | copy-start | bytes 1540
  40.0 4.8 %copy-start = (f32[3072]{0:T(1024)S(1)}, f32[3072]{0:T(1024)}, u32[]{:S(2)}) copy-start(f32[3072]{0:T(1024)} %param.16) | copy-start | bytes 36868
  44.7 122.0 %reduce-scatter.2.cloned.1.call-start = ((), (), s32[]{:S(2)}) async-start(), calls=%async_computation.3 | async-start | bytes 1572864 | tf_op jit(solution)/shard_map/reduce_scatter | solution.py:36
  44.9 123.1 %copy-start.3 = (s32[64]{0:T(128)S(1)}, s32[64]{0:T(128)}, u32[]{:S(2)}) copy-start(s32[64]{0:T(128)} %param.12) | copy-start | bytes 772
  145.0 13.7 %all-to-all-start = ((bf16[2,64,1536]{2,1,0:T(8,128)(2,1)}), bf16[2,64,1536]{2,1,0:T(8,128)(2,1)S(1)}, u32[]{:S(2)}, u32[]{:S(2)}) async-start(bf16[2,64,1536]{2,1,0:T(8,128)(2,1)} %bitcast.4), calls=%async_computation | async-start | bytes 786432 | tf_op jit(solution)/shard_map/all_to_all | solution.py:31
Sparse Core Ops, SparseCore 0:
  44.9 93.1 all-reduce.2
  145.1 21.6 reduce-scatter.1
where the time goes:
time: 208 us; the launch traced here: 207 us
  waiting for transfers between devices  111 us (53%)
  blocking collectives  56.8 us (27%)
  between operations  14.9 us (7%)
  matrix products  14.6 us (7%)
  other arithmetic  5.39 us (3%)
  starting transfers between devices  3.56 us (2%)
    psum x1, waiting for transfers between devices, per_device(): summed = lax.psum(part, ('expert', 'mp'))  93.2 us
    all_gather x1, blocking collectives, per_device(): lax.all_gather(jnp.stack([top, total, target_local]), ('expert', 'mp'))  30.6 us
    all_gather x1, blocking collectives, per_device(): all_tokens = lax.all_gather(tokens, 'dp', axis=0, tiled=True)  13.1 us
    all_to_all x1, waiting for transfers between devices, per_device(): lax.all_to_all(mixed_part, 'dp', split_axis=0, concat_axis=1, tiled=True)  10.2 us
    all_gather x1, blocking collectives, per_device(): hidden = lax.all_gather(hidden, 'dp', axis=1, tiled=True)  8.17 us
    reduce_scatter x1, waiting for transfers between devices, per_device(): lax.psum_scatter(logits_part, 'dp', scatter_dimension=0, tiled=True)  7.19 us
    unnamed x1, blocking collectives  4.92 us
    dot_general x1, matrix products, per_device(): logits_part = jnp.dot(gained, lens_head, preferred_element_type=f32)  4.91 us
  transfers between devices with their start and end apart: 3, of which 3 were waited for; matrix products, arithmetic and copies ran while one was open for 1% of the time, Pallas kernels for 0%

commit v1 on v0

--- a/solution.py
+++ b/solution.py
@@ -21,7 +21,14 @@
     gate_part = jnp.dot(all_tokens, gate_mat, preferred_element_type=f32)
     up_part = jnp.dot(all_tokens, up_mat, preferred_element_type=f32)
     hidden = (jax.nn.silu(gate_part) * up_part).astype(bf16)
-    hidden = lax.all_gather(hidden, "dp", axis=1, tiled=True)
+    ways, here, step = (lax.axis_size("dp"), lax.axis_index("dp"), hidden.shape[1])
+    line, have = (hidden, 1)
+    while have < ways:
+        line = jnp.concatenate(
+            [line, lax.ppermute(line, "dp", [(d, (d - have) % ways) for d in range(ways)])], axis=1
+        )
+        have = 2 * have
+    hidden = jnp.roll(line, here * step, axis=1)
     part = jnp.dot(hidden, down_mat, preferred_element_type=f32) * all_weights[:, None]
     summed = lax.psum(part, ("expert", "mp"))
     first = lax.axis_index("dp") * own_feats

time: 208 us -> 201 us (0.966)
  blocking collectives: 56.8 us -> 48.6 us
    all_gather x1 -> x0, blocking collectives: 8.17 us -> none  [per_device(): hidden = lax.all_gather(hidden, 'dp', axis=1, tiled=True)]
  transfers between devices with their start and end apart: 3 -> 4, of which waited for: 3 -> 3; matrix products, arithmetic and copies ran while one was open for 1% -> 1% of each run, Pallas kernels for 0% -> 0%
where the time goes in v1:
time: 201 us
  waiting for transfers between devices  110 us (55%)
  blocking collectives  48.6 us (24%)
  matrix products  14.9 us (7%)
  between operations  14.9 us (7%)
  other arithmetic  5.39 us (3%)
  starting transfers between devices  5.36 us (3%)
    psum x1, waiting for transfers between devices, per_device(): summed = lax.psum(part, ('expert', 'mp'))  92.6 us
    all_gather x1, blocking collectives, per_device(): lax.all_gather(jnp.stack([top, total, target_local]), ('expert', 'mp'))  30.6 us
    all_gather x1, blocking collectives, per_device(): all_tokens = lax.all_gather(tokens, 'dp', axis=0, tiled=True)  13.1 us
    all_to_all x1, waiting for transfers between devices, per_device(): lax.all_to_all(mixed_part, 'dp', split_axis=0, concat_axis=1, tiled=True)  10.2 us
    reduce_scatter x1, waiting for transfers between devices, per_device(): lax.psum_scatter(logits_part, 'dp', scatter_dimension=0, tiled=True)  7.19 us
    dot_general x1, matrix products, per_device(): jnp.dot(hidden, down_mat, preferred_element_type=f32) * all_weights[:, None]  5.01 us
    unnamed x1, blocking collectives  4.92 us
    dot_general x1, matrix products, per_device(): logits_part = jnp.dot(gained, lens_head, preferred_element_type=f32)  4.91 us
  transfers between devices with their start and end apart: 4, of which 3 were waited for; matrix products, arithmetic and copies ran while one was open for 1% of the time, Pallas kernels for 0%

profile of v1, /device:TPU:0, one launch (start us, length us, event | category | flops | bytes accessed | tf_op | source)
XLA Modules:
  0.0 200.8 jit_solution(7127057322932538795)
XLA Ops:
  7.2 0.0 all-reduce.3.cloned.1.call-start
  7.2 0.0 slice-start
  7.2 13.1 %all_gather.12 = bf16[128,3072]{1,0:T(8,128)(2,1)S(1)} all-gather(bf16[64,3072]{1,0:T(8,128)(2,1)} %param.9), channel_id=1, replica_groups=mesh['dp'=2,'expert'=4,'mp'=4] {'dp'}, dimensions={0}, use_global_device_ids=true | all-gather | bytes 1179648 | tf_op jit(solution)/shard_map/all_gather | solution.py:19
  20.3 3.9 %fusion.4 = f32[128,1024]{1,0:T(8,128)S(1)} fusion(bf16[128,3072]{1,0:T(8,128)(2,1)S(1)} %all_gather.12, bf16[1,3072,1,1024]{3,1,2,0:T(8,128)(2,1)} %param.13), kind=kOutput, calls=%fused_computation.4 | convolution fusion | flops 805306368 | bytes 7602176 | tf_op jit(solution)/shard_map/dot_general | solution.py:21
  24.3 0.0 copy-start.4
  24.3 0.0 copy-start.1
  24.3 0.0 copy-start.2
  24.3 1.1 fusion.12
  25.4 0.0 copy-start
  25.4 1.8 collective-permute-start
  27.2 0.0 copy-done.4
  27.2 0.6 dynamic-slice
  28.5 0.2 dynamic-update-slice
  28.7 4.9 %all-reduce = f32[128]{0:T(128)S(1)} all-reduce(f32[128]{0:T(128)S(1)} %dynamic-update-slice), channel_id=1, replica_groups=mesh['dp'=2,'expert'=4,'mp'=4] {'dp'}, use_global_device_ids=true, to_apply=%add | all-reduce | flops 128 | bytes 1024
  33.6 0.0 collective-permute-done
  33.6 5.0 %fusion.6 = f32[128,1536]{1,0:T(8,128)} fusion(bf16[1,1,2048,1536]{3,2,1,0:T(8,128)(2,1)} %param.15, s32[]{:T(128)S(6)} %select_n.27, bf16[128,1024]{1,0:T(8,128)(2,1)S(1)} %fusion.12, bf16[128,1024]{1,0:T(8,128)(2,1)S(1)} %collective-permute-done, f32[128]{0:T(128)S(1)} %all-reduce), kind=kOutput, calls=%fused_computation.6 | convolution fusion | flops 807600128 | bytes 7602692 | tf_op jit(solution)/shard_map/dot_general | solution.py:32
  38.7 0.0 all-reduce.3.cloned.1.call-update
  38.7 0.0 reduce-scatter.2.cloned.1.call-start
  38.7 0.1 dynamic_slice.12
  38.8 92.6 %all-reduce.3.cloned.1.call-done = f32[128,1536]{1,0:T(8,128)} async-done(((f32[128,1536]{1,0:T(8,128)}), f32[128,1536]{1,0:T(8,128)}) %all-reduce.3.cloned.1.call-update) | async-done | bytes 786448 | tf_op jit(solution)/shard_map/psum | solution.py:33
  131.5 1.9 add_convert_fusion
  133.4 4.9 %fusion.19 = f32[128,2048]{1,0:T(8,128)} fusion(bf16[1536,2048]{1,0:T(8,128)(2,1)} %param.17, bf16[128,1536]{1,0:T(8,128)(2,1)} %add_convert_fusion, f32[1536]{0:T(1024)S(1)} %dynamic_slice.12), kind=kOutput, calls=%fused_computation.22 | convolution fusion | flops 805896192 | bytes 7739392 | tf_op jit(solution)/shard_map/dot_general | solution.py:42
  138.3 0.0 reduce-scatter.2.cloned.1.call-update
  138.3 3.5 %all-to-all-start = ((bf16[2,64,1536]{2,1,0:T(8,128)(2,1)}), bf16[2,64,1536]{2,1,0:T(8,128)(2,1)S(1)}, u32[]{:S(2)}, u32[]{:S(2)}) async-start(bf16[2,64,1536]{2,1,0:T(8,128)(2,1)} %bitcast.4), calls=%async_computation | async-start | bytes 786432 | tf_op jit(solution)/shard_map/all_to_all | solution.py:38
  141.9 10.2 %all-to-all-done = bf16[2,64,1536]{2,1,0:T(8,128)(2,1)S(1)} async-done(((bf16[2,64,1536]{2,1,0:T(8,128)(2,1)}), bf16[2,64,1536]{2,1,0:T(8,128)(2,1)S(1)}, u32[]{:S(2)}, u32[]{:S(2)}) %all-to-all-start) | async-done | bytes 393248 | tf_op jit(solution)/shard_map/all_to_all | solution.py:38
  152.0 0.8 copy.16
  152.8 0.2 multiply_reduce_fusion
  153.0 7.2 %reduce-scatter.2.cloned.1.call-done = f32[64,2048]{1,0:T(8,128)} async-done(((f32[128,2048]{1,0:T(8,128)}), f32[64,2048]{1,0:T(8,128)}) %reduce-scatter.2.cloned.1.call-update) | async-done | bytes 524304 | tf_op jit(solution)/shard_map/reduce_scatter | solution.py:43
  160.2 1.2 multiply_reduce_fusion.1
  161.4 1.4 exponential_reduce_fusion
  162.8 30.6 %all-gather.1 = f32[16,3,64]{2,1,0:T(4,128)S(1)} all-gather(f32[1,3,64]{2,1,0:T(4,128)S(1)} %maximum_bitcast_fusion), channel_id=2, replica_groups=mesh['dp'=2,'expert'=4,'mp'=4] {'expert','mp'}, dimensions={0}, use_global_device_ids=true | all-gather | bytes 13056 | tf_op jit(solution)/shard_map/all_gather | solution.py:52
  193.5 0.5 log_subtract_fusion
  (16 shorter events, 0.1 us)
Async XLA Ops:
  7.2 124.3 %all-reduce.3.cloned.1.call-start = ((), (), s32[]{:S(2)}) async-start(), calls=%async_computation.2 | async-start | bytes 1572864 | tf_op jit(solution)/shard_map/psum | solution.py:33
  7.2 17.0 %slice-start = ((s8[6291456]{0:T(1024)(128)(4,1)}), s8[4194304]{0:T(1024)(128)(4,1)S(1)}, s32[]{:S(2)}) async-start(s8[6291456]{0:T(1024)(128)(4,1)} %bitcast.40), calls=%async_computation.4 | async-start | bytes 8388608
  20.3 3.9 %slice-start.1 = ((s8[6291456]{0:T(1024)(128)(4,1)}), s8[2097152]{0:T(1024)(128)(4,1)S(1)}, s32[]{:S(2)}) async-start(s8[6291456]{0:T(1024)(128)(4,1)} %bitcast.40), calls=%async_computation.5 | async-start | bytes 4194304
  24.3 3.0 %copy-start.4 = (u32[32]{0:T(128)S(1)}, u32[32]{0:T(128)}, u32[]{:S(2)}) copy-start(u32[32]{0:T(128)} %constant.62) | copy-start | bytes 388
  24.3 4.2 %copy-start.1 = (f32[64,2]{0,1:T(2,128)S(1)}, f32[64,2]{0,1:T(2,128)}, u32[]{:S(2)}) copy-start(f32[64,2]{0,1:T(2,128)} %param.11) | copy-start | bytes 1540
  24.3 4.2 %copy-start.2 = (s32[64,2]{0,1:T(2,128)S(1)}, s32[64,2]{0,1:T(2,128)}, u32[]{:S(2)}) copy-start(s32[64,2]{0,1:T(2,128)} %param.10) | copy-start | bytes 1540
  25.4 13.3 %copy-start = (f32[3072]{0:T(1024)S(1)}, f32[3072]{0:T(1024)}, u32[]{:S(2)}) copy-start(f32[3072]{0:T(1024)} %param.16) | copy-start | bytes 36868
  25.4 8.2 %collective-permute-start = (bf16[128,1024]{1,0:T(8,128)(2,1)S(1)}, bf16[128,1024]{1,0:T(8,128)(2,1)S(1)}, u32[]{:S(2)}, u32[]{:S(2)}) collective-permute-start(bf16[128,1024]{1,0:T(8,128)(2,1)S(1)} %fusion.12), channel_id=1, source_target_pairs={{0,16},{16,0},{1,17},{17,1},{2,18},{18,2},{3,19},{19,3},{4,20},{20... | collective-permute-start | bytes 786440 | tf_op jit(solution)/shard_map/ppermute | solution.py:28
  38.7 121.5 %reduce-scatter.2.cloned.1.call-start = ((), (), s32[]{:S(2)}) async-start(), calls=%async_computation.3 | async-start | bytes 1572864 | tf_op jit(solution)/shard_map/reduce_scatter | solution.py:43
  38.8 122.6 %copy-start.3 = (s32[64]{0:T(128)S(1)}, s32[64]{0:T(128)}, u32[]{:S(2)}) copy-start(s32[64]{0:T(128)} %param.12) | copy-start | bytes 772
  138.3 13.7 %all-to-all-start = ((bf16[2,64,1536]{2,1,0:T(8,128)(2,1)}), bf16[2,64,1536]{2,1,0:T(8,128)(2,1)S(1)}, u32[]{:S(2)}, u32[]{:S(2)}) async-start(bf16[2,64,1536]{2,1,0:T(8,128)(2,1)} %bitcast.4), calls=%async_computation | async-start | bytes 786432 | tf_op jit(solution)/shard_map/all_to_all | solution.py:38
Sparse Core Ops, SparseCore 0:
  38.8 92.6 all-reduce.2
  138.5 21.6 reduce-scatter.1
